TPU v7x, 256 devices: a whole 4x4x8 slice. The times are simulated.
256 devices in a mesh: ctx: 128 (over y, z, x), kvh: 2 (over core).
Axes of the slice: x: 4, y: 4, z: 8, core: 2. Of those that a mesh axis runs over, the one named last changes fastest.
Arguments:
- queries: bfloat16 [32768, 4096], P('ctx', 'kvh'), may hold values from -8 to 8
- current_keys: bfloat16 [32768, 1024], P('ctx', 'kvh'), may hold values from -8 to 8
- current_values: bfloat16 [32768, 1024], P('ctx', 'kvh'), may hold values from -6 to 6
- cached_key_pages: bfloat16 [524288, 1024], P('ctx', 'kvh'), may hold values from -8 to 8
- cached_value_pages: bfloat16 [524288, 1024], P('ctx', 'kvh'), may hold values from -6 to 6
- picks: int32 [128, 32, 3], P('ctx', 'kvh'), may hold values from 0 to 1023, as said below
Outputs:
- attended: bfloat16 [32768, 4096], P('ctx', 'kvh')
Inputs may be any that keep to these rules, and one draw needn't show every extreme that they name: Block n of the cache belongs to owner n // 8. For one query block and one set of 16 consecutive heads (h // 16 fixed), at most 1 of its 48 picks belong to one owner, and for each such set of heads one owner holds exactly 1 picks of every query block. The 3 picks of one query block and head belong to different owners.
All inputs are finite; a program needn't handle non-finite values.
Results may differ from a plain program's by a relative error of at most 0.0055.
Values may be sent and summed in bfloat16 or wider, within the bound.
A program may use at most 128 MiB of HBM per device.

v0:
```python
import jax
import jax.numpy as jnp
from jax import lax
from jax.sharding import PartitionSpec as P

HEAD_SIZE = 128
KEY_BLOCK_SIZE = 512
TOPK = 3


def from_behind(array, axis, by):
    count = lax.axis_size(axis)
    pairs = [(i, i + by) for i in range(count) if 0 <= i + by < count]
    return lax.ppermute(array, axis, pairs)


def local(queries, current_keys, current_values, cached_key_pages, cached_value_pages, picks):
    devices = lax.axis_size("ctx")
    query_rows = queries.shape[0]
    heads_here = queries.shape[1] // HEAD_SIZE
    kv_here = current_keys.shape[1] // HEAD_SIZE
    query_group_width = heads_here // kv_here
    blocks_here = cached_key_pages.shape[0] // KEY_BLOCK_SIZE
    unit_count = heads_here * TOPK
    slot_count = -(-unit_count // devices)
    score_scale = HEAD_SIZE ** (-0.5)
    chosen = picks.reshape(unit_count)
    owner_of = chosen // blocks_here
    within = chosen % blocks_here
    unit_ids = jnp.arange(unit_count)
    same_owner = owner_of[:, None] == owner_of[None, :]
    earlier = unit_ids[:, None] > unit_ids[None, :]
    slot_rank = jnp.sum(jnp.logical_and(same_owner, earlier).astype(jnp.int32), axis=1)
    slot_of = owner_of * slot_count + slot_rank
    placement = slot_of[None, :] == jnp.arange(devices * slot_count)[:, None]
    unit_head = unit_ids // TOPK
    head_pick = unit_head[:, None] == jnp.arange(heads_here)[None, :]
    head_select = jnp.dot(
        placement.astype(jnp.bfloat16),
        head_pick.astype(jnp.bfloat16),
        preferred_element_type=jnp.float32,
    ).astype(jnp.bfloat16)
    query_grid = queries.reshape(query_rows, heads_here, HEAD_SIZE)
    outgoing = jnp.einsum(
        "sh,qhd->sqd", head_select, query_grid, preferred_element_type=jnp.float32
    ).astype(jnp.bfloat16)
    outgoing = outgoing.reshape(devices, slot_count, query_rows, HEAD_SIZE)
    placed = placement.astype(jnp.int32)
    block_id = jnp.sum(placed * within[None, :], axis=1)
    kv_id = jnp.sum(placed * (unit_head // query_group_width)[None, :], axis=1)
    slot_meta = jnp.stack([block_id, kv_id], axis=-1).reshape(devices, slot_count, 2)
    table_k = (
        cached_key_pages.reshape(blocks_here, KEY_BLOCK_SIZE, kv_here, HEAD_SIZE)
        .transpose(2, 0, 1, 3)
        .reshape(kv_here * blocks_here, KEY_BLOCK_SIZE, HEAD_SIZE)
    )
    table_v = (
        cached_value_pages.reshape(blocks_here, KEY_BLOCK_SIZE, kv_here, HEAD_SIZE)
        .transpose(2, 0, 1, 3)
        .reshape(kv_here * blocks_here, KEY_BLOCK_SIZE, HEAD_SIZE)
    )
    previous_keys, previous_values = from_behind((current_keys, current_values), "ctx", 1)
    local_keys = jnp.concatenate([previous_keys, current_keys], axis=0).reshape(
        2 * query_rows, kv_here, HEAD_SIZE
    )
    local_values = jnp.concatenate([previous_values, current_values], axis=0).reshape(
        2 * query_rows, kv_here, HEAD_SIZE
    )
    grouped = queries.reshape(query_rows, kv_here, query_group_width, HEAD_SIZE)
    own_scores = (
        jnp.einsum("qkgd,tkd->kgqt", grouped, local_keys, preferred_element_type=jnp.float32)
        * score_scale
    )
    is_odd = lax.axis_index("ctx") % 2 == 1
    key_pos = jnp.arange(2 * query_rows)
    query_pos = jnp.arange(query_rows)
    visible = jnp.where(
        key_pos[None, :] < query_rows, is_odd, key_pos[None, :] - query_rows <= query_pos[:, None]
    )
    own_scores = jnp.where(visible[None, None], own_scores, -jnp.inf)
    own_max = jnp.max(own_scores, axis=-1)
    own_weights = jnp.where(visible[None, None], jnp.exp(own_scores - own_max[..., None]), 0.0)
    own_total = jnp.sum(own_weights, axis=-1)
    own_out = jnp.einsum(
        "kgqt,tkd->kgqd",
        own_weights.astype(jnp.bfloat16),
        local_values,
        preferred_element_type=jnp.float32,
    )
    own_out = (own_out / own_total[..., None]).reshape(heads_here, query_rows, HEAD_SIZE)
    own_max = own_max.reshape(heads_here, query_rows)
    own_total = own_total.reshape(heads_here, query_rows)
    received, slot_info = (
        lax.all_to_all(outgoing, "ctx", split_axis=0, concat_axis=0, tiled=True),
        lax.all_to_all(slot_meta, "ctx", split_axis=0, concat_axis=0, tiled=True),
    )
    count_src = received.shape[0]
    count_slot = received.shape[1]
    total_slots = count_src * count_slot
    batch_size = 8
    flat_queries = received.reshape(total_slots // batch_size, batch_size, query_rows, HEAD_SIZE)
    flat_index = (slot_info[..., 1] * blocks_here + slot_info[..., 0]).reshape(
        total_slots // batch_size, batch_size
    )

    def group_attend(inputs):
        query_part, index_part = inputs
        key_block = jnp.take(table_k, index_part, axis=0)
        value_block = jnp.take(table_v, index_part, axis=0)
        scores = (
            jnp.einsum("gqd,gkd->gqk", query_part, key_block, preferred_element_type=jnp.float32)
            * score_scale
        )
        row_max = jnp.max(scores, axis=-1)
        weights = jnp.exp(scores - row_max[..., None])
        row_total = jnp.sum(weights, axis=-1)
        partial_value = jnp.einsum(
            "gqk,gkd->gqd",
            weights.astype(jnp.bfloat16),
            value_block,
            preferred_element_type=jnp.float32,
        )
        partial_value = (partial_value / row_total[..., None]).astype(jnp.bfloat16)
        return (partial_value, row_max, row_total)

    part_out, part_max, part_total = lax.map(group_attend, (flat_queries, flat_index))
    part_out = part_out.reshape(count_src, count_slot, query_rows, HEAD_SIZE)
    part_max = part_max.reshape(count_src, count_slot, query_rows)
    part_total = part_total.reshape(count_src, count_slot, query_rows)
    part_out, part_max, part_total = (part_out, part_max, part_total)
    back_out = lax.all_to_all(part_out, "ctx", split_axis=0, concat_axis=0, tiled=True)
    back_max, back_total = (
        lax.all_to_all(part_max, "ctx", split_axis=0, concat_axis=0, tiled=True),
        lax.all_to_all(part_total, "ctx", split_axis=0, concat_axis=0, tiled=True),
    )
    pick_out = jnp.take(
        back_out.reshape(devices * slot_count, query_rows, HEAD_SIZE), slot_of, axis=0
    )
    pick_out = pick_out.reshape(heads_here, TOPK, query_rows, HEAD_SIZE).astype(jnp.float32)
    pick_max = jnp.take(
        back_max.reshape(devices * slot_count, query_rows), slot_of, axis=0
    ).reshape(heads_here, TOPK, query_rows)
    pick_total = jnp.take(
        back_total.reshape(devices * slot_count, query_rows), slot_of, axis=0
    ).reshape(heads_here, TOPK, query_rows)
    overall = jnp.maximum(own_max, jnp.max(pick_max, axis=1))
    own_weight = own_total * jnp.exp(own_max - overall)
    pick_weight = pick_total * jnp.exp(pick_max - overall[:, None])
    numer = own_weight[..., None] * own_out + jnp.sum(pick_weight[..., None] * pick_out, axis=1)
    result = numer / (own_weight + jnp.sum(pick_weight, axis=1))[..., None]
    return (
        result.transpose(1, 0, 2).reshape(query_rows, heads_here * HEAD_SIZE).astype(jnp.bfloat16)
    )


def solution(mesh):
    placed = (
        P("ctx", "kvh"),
        P("ctx", "kvh"),
        P("ctx", "kvh"),
        P("ctx", "kvh"),
        P("ctx", "kvh"),
        P("ctx", "kvh", None),
    )
    return jax.shard_map(
        local, mesh=mesh, in_specs=placed, out_specs=P("ctx", "kvh"), check_vma=False
    )
```

profile of v0, /device:TPU:30, one launch (start us, length us, event | category | flops | bytes accessed | tf_op | source)
XLA Modules:
  0.0 736.6 jit_solution(6926949936747138856)
XLA Ops:
  2.4 15.6 %all-to-all-start.1 = ((s32[128,1,2]{2,1,0:T(1,128)}), s32[128,1,2]{2,1,0:T(1,128)S(1)}, u32[]{:S(2)}, u32[]{:S(2)}) async-start(s32[128,1,2]{2,1,0:T(1,128)} %copy.70), calls=%async_computation.1 | async-start | bytes 131072 | tf_op jit(solution)/shard_map/all_to_all | solution.py:95
  19.5 5.1 convert_bitcast_fusion
  24.6 12.0 %copy.69 = bf16[128,1,256,128]{3,2,1,0:T(8,128)(2,1)} copy(bf16[128,1,256,128]{3,0,2,1:T(8,128)(2,1)} %convert_bitcast_fusion) | data formatting | bytes 16777216 | tf_op jit(solution)/shard_map/reshape | solution.py:47
  36.6 14.3 %all-to-all-start = ((bf16[128,1,256,128]{3,2,1,0:T(8,128)(2,1)}), bf16[128,1,256,128]{3,2,1,0:T(8,128)(2,1)}, u32[]{:S(2)}, u32[]{:S(2)}) async-start(bf16[128,1,256,128]{3,2,1,0:T(8,128)(2,1)} %copy.69), calls=%async_computation | async-start | bytes 16777216 | tf_op jit(solution)/shard_map/all_to_all | solution.py:94
  50.9 6.9 reshape.412
  57.8 5.1 copy.71
  62.9 6.9 reshape.414
  69.9 5.1 copy.72
  77.6 155.7 %all-to-all-done = bf16[128,1,256,128]{3,2,1,0:T(8,128)(2,1)} async-done(((bf16[128,1,256,128]{3,2,1,0:T(8,128)(2,1)}), bf16[128,1,256,128]{3,2,1,0:T(8,128)(2,1)}, u32[]{:S(2)}, u32[]{:S(2)}) %all-to-all-start) | async-done | bytes 8388640 | tf_op jit(solution)/shard_map/all_to_all | solution.py:94
  233.3 244.1 %while.14 = (s32[]{:T(128)}, bf16[16,8,256,128]{3,2,1,0:T(8,128)(2,1)}, f32[16,8,256]{2,1,0:T(8,128)S(1)}, f32[16,8,256]{2,1,0:T(8,128)S(1)}, bf16[16,8,256,128]...) while((s32[]{:T(128)}, ...), condition=%wide.region_8.10_spmd, body=%wide.region_5.9_spmd.sunk | while | flops 546829376 | bytes 36779320 | solution.py:126
  241.4 2.9 gather_fusion
  244.3 4.2 fusion.73
  256.6 2.9 gather_fusion
  259.6 4.2 fusion.73
  271.9 2.9 gather_fusion
  274.8 4.2 fusion.73
  287.2 2.9 gather_fusion
  290.1 4.2 fusion.73
  302.4 2.9 gather_fusion
  305.4 4.2 fusion.73
  317.7 2.9 gather_fusion
  320.6 4.2 fusion.73
  332.9 2.9 gather_fusion
  335.9 4.2 fusion.73
  348.2 2.9 gather_fusion
  351.1 4.2 fusion.73
  363.4 2.9 gather_fusion
  366.4 4.2 fusion.73
  378.7 2.9 gather_fusion
  381.6 4.2 fusion.73
  394.0 2.9 gather_fusion
  396.9 4.2 fusion.73
  409.2 2.9 gather_fusion
  412.2 4.2 fusion.73
  427.4 4.2 fusion.73
  442.7 4.2 fusion.73
  458.0 4.2 fusion.73
  473.2 4.2 fusion.73
  478.2 11.1 %all-to-all-start.3 = ((f32[128,1,256]{2,1,0:T(1,128)}), f32[128,1,256]{2,1,0:T(1,128)S(1)}, u32[]{:S(2)}, u32[]{:S(2)}) async-start(f32[128,1,256]{2,1,0:T(1,128)} %reshape.421), calls=%async_computation.3 | async-start | bytes 262144 | tf_op jit(solution)/shard_map/all_to_all | solution.py:134
  489.4 8.4 %all-to-all-done.3 = f32[128,1,256]{2,1,0:T(1,128)S(1)} async-done(((f32[128,1,256]{2,1,0:T(1,128)}), f32[128,1,256]{2,1,0:T(1,128)S(1)}, u32[]{:S(2)}, u32[]{:S(2)}) %all-to-all-start.3) | async-done | bytes 131104 | tf_op jit(solution)/shard_map/all_to_all | solution.py:134
  497.8 17.8 %all_to_all.25 = f32[128,1,256]{2,1,0:T(1,128)S(1)} all-to-all(f32[128,1,256]{2,1,0:T(1,128)S(1)} %reshape.416), channel_id=1, replica_groups=mesh['ctx'=128,'kvh'=2] {'ctx'}, dimensions={0} | all-to-all | bytes 262144 | tf_op jit(solution)/shard_map/all_to_all | solution.py:133
  515.6 11.4 %all-to-all-start.4 = ((bf16[128,1,256,128]{3,2,1,0:T(8,128)(2,1)}), bf16[128,1,256,128]{3,2,1,0:T(8,128)(2,1)}, u32[]{:S(2)}, u32[]{:S(2)}) async-start(bf16[128,1,256,128]{3,2,1,0:T(8,128)(2,1)} %bitcast.109), calls=%async_computation.4 | async-start | bytes 16777216 | tf_op jit(solution)/shard_map/all_to_all | solution.py:131
  527.2 3.4 collective-permute-start
  530.6 3.4 collective-permute-start.1
  536.6 173.7 %collective-permute-done = bf16[256,512]{0,1:T(8,128)(2,1)S(1)} collective-permute-done((bf16[256,512]{0,1:T(8,128)(2,1)S(1)}, bf16[256,512]{0,1:T(8,128)(2,1)S(1)}, u32[]{:S(2)}, u32[]{:S(2)}) %collective-permute-start) | collective-permute-done | bytes 262176 | tf_op jit(solution)/shard_map/ppermute | solution.py:14
  712.0 3.2 copy-done.1
  717.5 5.6 broadcast_divide_fusion
  726.7 4.5 gather_fusion.2
  (202 shorter events, 164.1 us)
Async XLA Ops:
  2.4 34.1 %all-to-all-start.1 = ((s32[128,1,2]{2,1,0:T(1,128)}), s32[128,1,2]{2,1,0:T(1,128)S(1)}, u32[]{:S(2)}, u32[]{:S(2)}) async-start(s32[128,1,2]{2,1,0:T(1,128)} %copy.70), calls=%async_computation.1 | async-start | bytes 131072 | tf_op jit(solution)/shard_map/all_to_all | solution.py:95
  36.6 196.7 %all-to-all-start = ((bf16[128,1,256,128]{3,2,1,0:T(8,128)(2,1)}), bf16[128,1,256,128]{3,2,1,0:T(8,128)(2,1)}, u32[]{:S(2)}, u32[]{:S(2)}) async-start(bf16[128,1,256,128]{3,2,1,0:T(8,128)(2,1)} %copy.69), calls=%async_computation | async-start | bytes 16777216 | tf_op jit(solution)/shard_map/all_to_all | solution.py:94
  238.1 2.0 copy-start
  253.4 2.0 copy-start
  268.6 2.0 copy-start
  283.9 2.0 copy-start
  299.2 2.0 copy-start
  314.4 2.0 copy-start
  329.7 2.0 copy-start
  344.9 2.0 copy-start
  360.2 2.0 copy-start
  375.4 2.0 copy-start
  390.7 2.0 copy-start
  406.0 2.0 copy-start
  421.2 2.0 copy-start
  436.5 2.0 copy-start
  451.8 2.0 copy-start
  467.0 2.0 copy-start
  478.2 19.6 %all-to-all-start.3 = ((f32[128,1,256]{2,1,0:T(1,128)}), f32[128,1,256]{2,1,0:T(1,128)S(1)}, u32[]{:S(2)}, u32[]{:S(2)}) async-start(f32[128,1,256]{2,1,0:T(1,128)} %reshape.421), calls=%async_computation.3 | async-start | bytes 262144 | tf_op jit(solution)/shard_map/all_to_all | solution.py:134
  515.6 11.5 %copy-start.4 = (bf16[256,512]{1,0:T(8,128)(2,1)S(1)}, bf16[256,512]{1,0:T(8,128)(2,1)}, u32[]{:S(2)}) copy-start(bf16[256,512]{1,0:T(8,128)(2,1)} %param.13) | copy-start | bytes 786436
  515.6 15.0 %copy-start.5 = (bf16[256,512]{1,0:T(8,128)(2,1)S(1)}, bf16[256,512]{1,0:T(8,128)(2,1)}, u32[]{:S(2)}) copy-start(bf16[256,512]{1,0:T(8,128)(2,1)} %param.14) | copy-start | bytes 786436
  515.6 18.7 %copy-start.6 = (s32[1,16,3]{1,0,2:T(1,128)S(1)}, s32[1,16,3]{1,0,2:T(1,128)}, u32[]{:S(2)}) copy-start(s32[1,16,3]{1,0,2:T(1,128)} %param.17) | copy-start | bytes 580
  515.6 19.2 %copy-start.3 = (bf16[256,2048]{1,0:T(8,128)(2,1)S(1)}, bf16[256,2048]{1,0:T(8,128)(2,1)}, u32[]{:S(2)}) copy-start(bf16[256,2048]{1,0:T(8,128)(2,1)} %param.12) | copy-start | bytes 3145732
  515.6 211.0 %all-to-all-start.4 = ((bf16[128,1,256,128]{3,2,1,0:T(8,128)(2,1)}), bf16[128,1,256,128]{3,2,1,0:T(8,128)(2,1)}, u32[]{:S(2)}, u32[]{:S(2)}) async-start(bf16[128,1,256,128]{3,2,1,0:T(8,128)(2,1)} %bitcast.109), calls=%async_computation.4 | async-start | bytes 16777216 | tf_op jit(solution)/shard_map/all_to_all | solution.py:131
  527.2 183.1 %collective-permute-start = (bf16[256,512]{0,1:T(8,128)(2,1)S(1)}, bf16[256,512]{0,1:T(8,128)(2,1)S(1)}, u32[]{:S(2)}, u32[]{:S(2)}) collective-permute-start(bf16[256,512]{0,1:T(8,128)(2,1)S(1)} %copy.64), channel_id=1, source_target_pairs={{0,2},{2,4},{4,6},{6,8},{8,10},{10,12},{12,14},{14,16},{16,18},{18... | collective-permute-start | bytes 786440 | tf_op jit(solution)/shard_map/ppermute | solution.py:14
  530.6 186.6 %collective-permute-start.1 = (bf16[256,512]{1,0:T(8,128)(2,1)S(1)}, bf16[256,512]{1,0:T(8,128)(2,1)S(1)}, u32[]{:S(2)}, u32[]{:S(2)}) collective-permute-start(bf16[256,512]{1,0:T(8,128)(2,1)S(1)} %copy-done.5), channel_id=1, source_target_pairs={{0,2},{2,4},{4,6},{6,8},{8,10},{10,12},{12,14},{14,16},{16,18},{18... | collective-permute-start | bytes 786440 | tf_op jit(solution)/shard_map/ppermute | solution.py:14
  712.0 3.2 copy-start.1
  723.1 3.2 copy-start.7
  731.2 2.2 copy-start.2
where the time goes:
time: 745 us; the launch traced here: 737 us
  waiting for transfers between devices  338 us (45%)
  local copies, waits for them, and re-layouts  180 us (24%)
  matrix products  110 us (15%)
  starting transfers between devices  59.1 us (8%)
  other arithmetic  30.9 us (4%)
  blocking collectives  17.8 us (2%)
    ppermute x2, waiting for transfers between devices, from_behind(): return lax.ppermute(array, axis, pairs)  174 us
    all_to_all x1, waiting for transfers between devices, local(): lax.all_to_all(outgoing, 'ctx', split_axis=0, concat_axis=0, tiled=True)  156 us
    dot_general x16, matrix products, group_attend(): jnp.einsum('gqk,gkd->gqd', weights.astype(jnp.bfloat16), value_block, pre...  67.1 us
    gather x16, local copies, waits for them, and re-layouts, group_attend(): value_block = jnp.take(table_v, index_part, axis=0)  47 us
    gather x16, local copies, waits for them, and re-layouts, group_attend(): key_block = jnp.take(table_k, index_part, axis=0)  47 us
    while x32, local copies, waits for them, and re-layouts  31.6 us
    dot_general x16, matrix products, group_attend(): jnp.einsum('gqd,gkd->gqk', query_part, key_block, preferred_element_type=...  30.5 us
    reduce_sum x16, other arithmetic, group_attend(): row_total = jnp.sum(weights, axis=-1)  20.1 us
  transfers between devices with their start and end apart: 6, of which 3 were waited for; matrix products, arithmetic and copies ran while one was open for 8% of the time, Pallas kernels for 0%

commit v1 on v0

v1 whole, which is shorter than its diff:
```python
import functools

import jax
import jax.numpy as jnp
from jax import lax
from jax.experimental import pallas as pl
from jax.experimental.pallas import tpu as pltpu
from jax.sharding import PartitionSpec as P

HEAD_SIZE = 128
KEY_BLOCK_SIZE = 512
TOPK = 3
MESH = pl.DeviceIdType.MESH
NX, NY, NZ = 4, 4, 8
PLANE = NX * NY
HEADS = 16
KV = 4
GROUP = HEADS // KV
OWNED = 8
ROWS = 256
HALF = 128
OWNERS = 128
SCALE = HEAD_SIZE**-0.5
SCALE2 = SCALE * 1.4426950408889634
LOW = -1e30


def kernel(*refs):
    (q_ref, ck_ref, cv_ref, kp_ref, vp_ref, code_ref, out_ref), refs = refs[:7], refs[7:]
    zq, refs = [refs[2 * s : 2 * s + 2] for s in range(NZ)], refs[2 * NZ :]
    ret, refs = [refs[2 * s : 2 * s + 2] for s in range(NZ)], refs[2 * NZ :]
    rl, refs = refs[:NZ], refs[NZ:]
    (
        kbuf, vstage, vbuf, tx, rx, lout, zacc, zl, own_o, own_l, pk, pvt, cvt, lt, wt,
        zcode, pcode, zsm, rsm,
        k_sem, v_sem, zq_send, zq_recv, zc_send, zc_recv, pc_send, pc_recv, sm_sem,
        xp_send, xp_recv, tx_send, rx_recv, rs_send, rs_recv, ls_send, ls_recv,
        za_send, za_recv, zl_send, zl_recv,
    ) = refs
    me = lax.axis_index("ctx")
    core = lax.axis_index("kvh")
    x = lax.rem(me, NX)
    z = lax.rem(me // NX, NZ)
    y = me // (NX * NZ)

    def in_plane(k):
        return (
            lax.rem(y + k // NX, NY) * (NX * NZ) + z * NX + lax.rem(x + lax.rem(k, NX), NX),
            core,
        )

    def opposite(k):
        return (
            lax.rem(y + NY - k // NX, NY) * (NX * NZ)
            + z * NX
            + lax.rem(x + NX - lax.rem(k, NX), NX),
            core,
        )

    def along_z(d):
        return (y * (NX * NZ) + lax.rem(z + d + NZ, NZ) * NX + x, core)

    def owner_at(k):
        return in_plane(k)[0]

    def remote(src, dst, send, recv, device):
        return pltpu.make_async_remote_copy(
            src_ref=src,
            dst_ref=dst,
            send_sem=send,
            recv_sem=recv,
            device_id=device,
            device_id_type=MESH,
        )

    def key_copy(v):
        return pltpu.make_async_copy(
            kp_ref.at[:, :, pl.ds(v * HEAD_SIZE, HEAD_SIZE)],
            kbuf.at[pl.ds(v * OWNED, OWNED)],
            k_sem.at[v],
        )

    def value_copy(v):
        return pltpu.make_async_copy(
            vp_ref.at[:, :, pl.ds(v * HEAD_SIZE, HEAD_SIZE)], vstage.at[v % 2], v_sem.at[v]
        )

    value_copy(0).start()
    value_copy(1).start()
    for v in range(KV):
        key_copy(v).start()

    barrier = pltpu.get_barrier_semaphore()
    for k in range(1, PLANE):
        pl.semaphore_signal(barrier, inc=1, device_id=in_plane(k), device_id_type=MESH)
    for d in range(1, NZ):
        pl.semaphore_signal(barrier, inc=1, device_id=along_z(d), device_id_type=MESH)
    pl.semaphore_wait(barrier, PLANE - 1 + NZ - 1)

    zcode[0] = code_ref[...]

    def z_code(d):
        return remote(zcode.at[0], zcode.at[d], zc_send, zc_recv, along_z(d))

    for d in range(1, NZ):
        z_code(d).start()

    def z_query(s, c, to, step):
        return remote(
            zq[s][c], zq[to][c], zq_send.at[0 if step > 0 else 1, s, c], zq_recv.at[to, c],
            along_z(step),
        )

    for c in range(2):
        for h in range(HEADS):
            zq[0][c][h] = q_ref[
                c * HALF : (c + 1) * HALF, h * HEAD_SIZE : (h + 1) * HEAD_SIZE
            ].T
        z_query(0, c, 1, 1).start()
        z_query(0, c, NZ - 1, -1).start()

    for v in range(KV):
        cvt[v] = cv_ref[:, v * HEAD_SIZE : (v + 1) * HEAD_SIZE].T
    odd = lax.rem(me, 2)
    partner = (me + 1 - 2 * odd, core)
    pair = [
        remote(ck_ref, pk, xp_send.at[0], xp_recv.at[0], partner),
        remote(cvt, pvt, xp_send.at[1], xp_recv.at[1], partner),
    ]
    for copy in pair:
        copy.start()

    z_codes = remote(
        zcode.at[pl.ds(1, NZ - 1)], zcode.at[pl.ds(1, NZ - 1)], zc_send, zc_recv, along_z(1)
    )
    z_codes.wait_recv()

    def p_code(k):
        return remote(
            zcode.at[:, :, pl.ds(0, OWNERS)], pcode.at[k], pc_send, pc_recv, in_plane(k)
        )

    def start_p_code(k, _):
        p_code(k).start()
        return 0

    lax.fori_loop(1, PLANE, start_p_code, 0)
    pcode[0] = zcode[:, :, :OWNERS]
    z_to_smem = pltpu.make_async_copy(zcode, zsm, sm_sem.at[0])
    z_to_smem.start()
    z_to_smem.wait()

    def query_copy(s, c, k):
        return remote(
            tx.at[s, c, k], rx.at[s, c, k], tx_send.at[s], rx_recv.at[s, c, k], in_plane(k)
        )

    def send_out(s, c):
        first = lax.rem(zsm[s, 0, owner_at(0)], HEADS)
        rx[s, c, 0] = zq[s][c][first]

        def body(k, _):
            head = lax.rem(zsm[s, 0, owner_at(k)], HEADS)
            tx[s, c, k] = zq[s][c][head]
            query_copy(s, c, k).start()
            return 0

        lax.fori_loop(1, PLANE, body, 0)

    def pass_on(s, c):
        remote(zq[s][c], zq[s][c], zq_send.at[0, s, c], zq_recv.at[s, c], along_z(1)).wait_recv()
        if s < NZ // 2 - 1 or (s == NZ // 2 - 1 and c == 0):
            z_query(s, c, s + 1, 1).start()
        elif s > NZ // 2 + 1 or (s == NZ // 2 + 1 and c == 1):
            z_query(s, c, s - 1, -1).start()

    def arrive(*pairs):
        for s, c in pairs:
            pass_on(s, c)
        for s, c in pairs:
            send_out(s, c)

    def attend(keys, queries, values):
        scores = jnp.dot(keys, queries, preferred_element_type=jnp.float32)
        top = jnp.max(scores, axis=0, keepdims=True)
        weights = jnp.exp2(scores * SCALE2 - top * SCALE2)
        total = jnp.sum(weights, axis=0, keepdims=True)
        out = jnp.dot(values, weights.astype(jnp.bfloat16), preferred_element_type=jnp.float32)
        return out * (1.0 / total), top * SCALE + jnp.log(total)

    def unit(s, k):
        table = lax.div(rsm[k, s, 0, me], HEADS)
        queries = jnp.concatenate([rx[s, 0, k], rx[s, 1, k]], axis=1)
        out, level = attend(kbuf[table], queries, vbuf[table])
        out = out.astype(jnp.bfloat16)
        rx[s, 0, k] = out[:, :HALF]
        rx[s, 1, k] = out[:, HALF:]
        lout[s, k] = level

    def back_copy(s, c, k):
        return remote(
            rx.at[s, c, k], ret[s][c].at[k], rs_send.at[s], rs_recv.at[s, c], opposite(k)
        )

    def level_copy(s, k):
        return remote(lout.at[s, k], rl[s].at[k], ls_send.at[s], ls_recv.at[s], opposite(k))

    def units(a, b, count, then=None):
        def body(j, _):
            s = a + (b - a) * lax.div(j, PLANE // 2)
            for i in range(2):
                k = lax.rem(j, PLANE // 2) * 2 + i

                def wait(k=k):
                    query_copy(s, 0, k).wait_recv()
                    query_copy(s, 1, k).wait_recv()

                if i == 0:
                    pl.when(k > 0)(wait)
                else:
                    wait()
            for i in range(2):
                unit(s, lax.rem(j, PLANE // 2) * 2 + i)
            if then is not None:
                for i in range(2):
                    then(lax.rem(j, PLANE // 2) * 2 + i, i)
            return 0

        lax.fori_loop(0, count * PLANE // 2, body, 0)
        for s in (a, b)[:count]:
            for c in range(2):
                ret[s][c][0] = rx[s, c, 0]
            rl[s][0] = lout[s, 0]
            rl[s][PLANE] = jnp.full((1, ROWS), LOW, jnp.float32)

    def send_back(s, c, with_level):
        def body(k, _):
            back_copy(s, c, k).start()
            if with_level:
                level_copy(s, k).start()
            return 0

        lax.fori_loop(1, PLANE, body, 0)

    send_out(0, 0)
    send_out(0, 1)

    for v in range(KV):
        value_copy(v).wait()

        def turn(w, _, v=v):
            vbuf[v * OWNED + w] = vstage[v % 2, w].T
            return 0

        lax.fori_loop(0, OWNED, turn, 0)
        if v + 2 < KV:
            value_copy(v + 2).start()

    arrive((1, 0), (7, 0))

    for copy in pair:
        copy.wait_recv()

    def own(h, _):
        v = h // GROUP
        lanes = pl.ds(pl.multiple_of(v * HEAD_SIZE, HEAD_SIZE), HEAD_SIZE)
        queries = jnp.concatenate([zq[0][0][h], zq[0][1][h]], axis=1)
        before = jnp.dot(pk[:, lanes], queries, preferred_element_type=jnp.float32)
        here = jnp.dot(ck_ref[:, lanes], queries, preferred_element_type=jnp.float32)
        key_pos = lax.broadcasted_iota(jnp.int32, (ROWS, ROWS), 0)
        query_pos = lax.broadcasted_iota(jnp.int32, (ROWS, ROWS), 1)
        before = jnp.where(odd == 1, before, LOW)
        here = jnp.where(key_pos <= query_pos, here, LOW)
        top = jnp.maximum(
            jnp.max(before, axis=0, keepdims=True), jnp.max(here, axis=0, keepdims=True)
        )
        weights_before = jnp.exp2((before - top) * SCALE2)
        weights_here = jnp.exp2((here - top) * SCALE2)
        total = jnp.sum(weights_before, axis=0, keepdims=True) + jnp.sum(
            weights_here, axis=0, keepdims=True
        )
        out = jnp.dot(pvt[v], weights_before.astype(jnp.bfloat16), preferred_element_type=jnp.float32)
        out += jnp.dot(cvt[v], weights_here.astype(jnp.bfloat16), preferred_element_type=jnp.float32)
        out = out * (1.0 / total)
        level = top * SCALE + jnp.log(total)
        for c in range(2):
            own_o[c, h] = out[:, c * HALF : (c + 1) * HALF]
            own_l[c, pl.ds(h, 1), :] = level[:, c * HALF : (c + 1) * HALF]
        return 0

    lax.fori_loop(0, HEADS, own, 0)
    arrive((1, 1), (7, 1))

    remote(
        pcode.at[pl.ds(1, PLANE - 1)], pcode.at[pl.ds(1, PLANE - 1)], pc_send, pc_recv, in_plane(1)
    ).wait_recv()
    p_to_smem = pltpu.make_async_copy(pcode, rsm, sm_sem.at[1])
    p_to_smem.start()
    p_to_smem.wait()
    for v in range(KV):
        key_copy(v).wait()

    units(0, 0, 1)
    arrive((2, 0), (6, 0))
    arrive((2, 1), (6, 1))
    units(1, 7, 2)
    arrive((3, 0), (5, 0))
    arrive((3, 1), (5, 1))
    units(2, 6, 2)
    arrive((4, 0), (4, 1))
    units(3, 5, 2)

    def back_now(k, i):
        def start():
            level_copy(4, k).start()
            back_copy(4, 0, k).start()
            back_copy(4, 1, k).start()

        if i == 0:
            pl.when(k > 0)(start)
        else:
            start()

    units(4, 4, 1, back_now)

    def pick(s, h, t):
        owner = zsm[s, 0, OWNERS + h * TOPK + t]
        dx = lax.rem(lax.rem(owner, NX) - x + NX, NX)
        dy = lax.rem(lax.div(owner, NX * NZ) - y + NY, NY)
        dz = lax.rem(lax.rem(lax.div(owner, NX), NZ) - z + NZ, NZ)
        away = lax.div(dz + NZ - 1, NZ)
        return away, (dx + NX * dy) * (1 - away)

    def gather_levels(s):
        remote(
            rl[s].at[pl.ds(1, PLANE - 1)], rl[s].at[pl.ds(1, PLANE - 1)],
            ls_send.at[s], ls_recv.at[s], in_plane(1),
        ).wait_recv()

        def body(h, _):
            for t in range(TOPK):
                away, k = pick(s, h, t)
                lt[s, t, pl.ds(h, 1), :] = rl[s][k + PLANE * away]
            return 0

        lax.fori_loop(0, HEADS, body, 0)

    def weigh(c, levels):
        top = functools.reduce(jnp.maximum, levels)
        parts = [jnp.exp(level - top) for level in levels]
        total = functools.reduce(jnp.add, parts)
        inverse = 1.0 / total
        for i, part in enumerate(parts):
            wt[c, i] = part * inverse
        return top + jnp.log(total)

    def picked_levels(s, c):
        return [lt[s, t, :, c * HALF : (c + 1) * HALF] for t in range(TOPK)]

    def picked_sum(s, c, h):
        total = None
        for t in range(TOPK):
            _, k = pick(s, h, t)
            term = wt[c, t, pl.ds(h, 1), :] * ret[s][c][k].astype(jnp.float32)
            total = term if total is None else total + term
        return total

    def wait_back(s, c):
        remote(
            ret[s][c].at[pl.ds(1, PLANE - 1)], ret[s][c].at[pl.ds(1, PLANE - 1)],
            rs_send.at[s], rs_recv.at[s, c], in_plane(1),
        ).wait_recv()

    def wait_sum(s, c):
        remote(
            zacc.at[s, c], zacc.at[s, c], za_send.at[0, c], za_recv.at[s, c], along_z(1)
        ).wait_recv()
        remote(
            zl.at[s, c], zl.at[s, c], zl_send.at[0, c], zl_recv.at[s, c], along_z(1)
        ).wait_recv()

    def sum_copies(s, c):
        down = s < NZ // 2 or (s == NZ // 2 and c == 0)
        to, step = (s - 1, -1) if down else (s + 1, 1)
        return [
            remote(
                zacc.at[s, c], zacc.at[to, c], za_send.at[s, c], za_recv.at[to, c], along_z(step)
            ),
            remote(zl.at[s, c], zl.at[to, c], zl_send.at[s, c], zl_recv.at[to, c], along_z(step)),
        ]

    def combine(s, c):
        upstream = s != NZ // 2 and (s, c) not in ((NZ // 2 - 1, 1), (NZ // 2 + 1, 0))
        wait_back(s, c)
        levels = picked_levels(s, c)
        if upstream:
            wait_sum(s, c)
            levels.append(zl[s, c])
        zl[s, c] = weigh(c, levels)

        def body(h, _):
            total = picked_sum(s, c, h)
            if upstream:
                total += wt[c, TOPK, pl.ds(h, 1), :] * zacc[s, c, h].astype(jnp.float32)
            zacc[s, c, h] = total.astype(jnp.bfloat16)
            return 0

        lax.fori_loop(0, HEADS, body, 0)
        for copy in sum_copies(s, c):
            copy.start()

    for s, c in ((5, 0), (3, 1), (5, 1), (3, 0)):
        send_back(s, c, (s, c) in ((5, 0), (3, 1)))
    gather_levels(4)
    combine(4, 0)
    combine(4, 1)
    for up, down in ((5, 3), (6, 2), (7, 1)):
        if up < 7:
            for s, c in ((up + 1, 0), (down - 1, 1), (up + 1, 1), (down - 1, 0)):
                send_back(s, c, (s, c) in ((up + 1, 0), (down - 1, 1)))
        else:
            send_back(0, 0, True)
            send_back(0, 1, False)
        gather_levels(up)
        combine(up, 0)
        gather_levels(down)
        combine(down, 1)
        combine(up, 1)
        combine(down, 0)

    gather_levels(0)
    for c in range(2):
        wait_back(0, c)
        wait_sum(0, c)
        wait_sum(NZ, c)
        weigh(c, picked_levels(0, c) + [zl[0, c], zl[NZ, c], own_l[c]])

        def finish(h, _, c=c):
            total = picked_sum(0, c, h)
            total += wt[c, TOPK, pl.ds(h, 1), :] * zacc[0, c, h].astype(jnp.float32)
            total += wt[c, TOPK + 1, pl.ds(h, 1), :] * zacc[NZ, c, h].astype(jnp.float32)
            total += wt[c, TOPK + 2, pl.ds(h, 1), :] * own_o[c, h]
            lanes = pl.ds(pl.multiple_of(h * HEAD_SIZE, HEAD_SIZE), HEAD_SIZE)
            out_ref[c * HALF : (c + 1) * HALF, lanes] = total.T.astype(jnp.bfloat16)
            return 0

        lax.fori_loop(0, HEADS, finish, 0)

    z_codes.wait_send()
    remote(
        pcode.at[pl.ds(1, PLANE - 1)], pcode.at[pl.ds(1, PLANE - 1)], pc_send, pc_recv, in_plane(1)
    ).wait_send()
    for copy in pair:
        copy.wait_send()
    half = NZ // 2
    for c in range(2):
        for s in range(NZ):
            if s < half - 1 or (s == half - 1 and c == 0):
                z_query(s, c, s + 1, 1).wait_send()
            if s == 0 or s > half + 1 or (s == half + 1 and c == 1):
                z_query(s, c, (s - 1) % NZ, -1).wait_send()
            if s > 0:
                for copy in sum_copies(s, c):
                    copy.wait_send()
    others = pl.ds(1, PLANE - 1)
    for s in range(NZ):
        remote(
            tx.at[s, :, others], rx.at[s, :, others], tx_send.at[s], rx_recv.at[s, 0, 0], in_plane(1)
        ).wait_send()
        remote(
            rx.at[s, :, others], tx.at[s, :, others], rs_send.at[s], rs_recv.at[s, 0], in_plane(1)
        ).wait_send()
        remote(
            lout.at[s, others], rl[s].at[others], ls_send.at[s], ls_recv.at[s], in_plane(1)
        ).wait_send()


def exchange(q, ck, cv, kp, vp, code):
    dma = pltpu.SemaphoreType.DMA
    bf16, f32 = jnp.bfloat16, jnp.float32
    half = (HEADS, HEAD_SIZE, HALF)
    scratch = [pltpu.VMEM(half, bf16)] * (2 * NZ)
    scratch += [pltpu.VMEM((PLANE, HEAD_SIZE, HALF), bf16)] * (2 * NZ)
    scratch += [pltpu.VMEM((PLANE + 1, 1, ROWS), f32)] * NZ
    scratch += [
        pltpu.VMEM((KV * OWNED, KEY_BLOCK_SIZE, HEAD_SIZE), bf16),
        pltpu.VMEM((2, OWNED, KEY_BLOCK_SIZE, HEAD_SIZE), bf16),
        pltpu.VMEM((KV * OWNED, HEAD_SIZE, KEY_BLOCK_SIZE), bf16),
        pltpu.VMEM((NZ, 2, PLANE, HEAD_SIZE, HALF), bf16),
        pltpu.VMEM((NZ, 2, PLANE, HEAD_SIZE, HALF), bf16),
        pltpu.VMEM((NZ, PLANE, 1, ROWS), f32),
        pltpu.VMEM((NZ + 1, 2) + half, bf16),
        pltpu.VMEM((NZ + 1, 2, HEADS, HALF), f32),
        pltpu.VMEM((2,) + half, f32),
        pltpu.VMEM((2, HEADS, HALF), f32),
        pltpu.VMEM((ROWS, KV * HEAD_SIZE), bf16),
        pltpu.VMEM((KV, HEAD_SIZE, ROWS), bf16),
        pltpu.VMEM((KV, HEAD_SIZE, ROWS), bf16),
        pltpu.VMEM((NZ, TOPK, HEADS, ROWS), f32),
        pltpu.VMEM((2, TOPK + 3, HEADS, HALF), f32),
        pltpu.VMEM((NZ, 1, 2 * OWNERS), jnp.int32),
        pltpu.VMEM((PLANE, NZ, 1, OWNERS), jnp.int32),
        pltpu.SMEM((NZ, 1, 2 * OWNERS), jnp.int32),
        pltpu.SMEM((PLANE, NZ, 1, OWNERS), jnp.int32),
        dma((KV,)), dma((KV,)),
        dma((2, NZ, 2)), dma((NZ, 2)),
        dma, dma, dma, dma, dma((2,)),
        dma((2,)), dma((2,)),
        dma((NZ,)), dma((NZ, 2, PLANE)),
        dma((NZ,)), dma((NZ, 2)),
        dma((NZ,)), dma((NZ,)),
        dma((NZ, 2)), dma((NZ + 1, 2)), dma((NZ, 2)), dma((NZ + 1, 2)),
    ]
    vmem = pl.BlockSpec(memory_space=pltpu.VMEM)
    hbm = pl.BlockSpec(memory_space=pl.ANY)
    return pl.pallas_call(
        kernel,
        out_shape=jax.ShapeDtypeStruct((ROWS, HEADS * HEAD_SIZE), bf16),
        in_specs=[vmem, vmem, vmem, hbm, hbm, vmem],
        out_specs=vmem,
        scratch_shapes=scratch,
        compiler_params=pltpu.CompilerParams(
            collective_id=0, has_side_effects=True, vmem_limit_bytes=62 << 20
        ),
        name="attend",
    )(q, ck, cv, kp, vp, code)


def local(queries, current_keys, current_values, cached_key_pages, cached_value_pages, picks):
    chosen = picks.reshape(HEADS * TOPK)
    owner = chosen // OWNED
    head = jnp.arange(HEADS * TOPK) // TOPK
    table = head // GROUP * OWNED + chosen % OWNED
    value = head + HEADS * table
    by_owner = jnp.sum(
        jnp.where(owner[None, :] == jnp.arange(OWNERS)[:, None], value[None, :], 0), axis=1
    )
    code = jnp.concatenate([by_owner, jnp.pad(owner, (0, OWNERS - HEADS * TOPK))])
    return exchange(
        queries,
        current_keys,
        current_values,
        cached_key_pages.reshape(OWNED, KEY_BLOCK_SIZE, KV * HEAD_SIZE),
        cached_value_pages.reshape(OWNED, KEY_BLOCK_SIZE, KV * HEAD_SIZE),
        code.reshape(1, 2 * OWNERS).astype(jnp.int32),
    )


def solution(mesh):
    placed = (
        P("ctx", "kvh"),
        P("ctx", "kvh"),
        P("ctx", "kvh"),
        P("ctx", "kvh"),
        P("ctx", "kvh"),
        P("ctx", "kvh", None),
    )
    return jax.shard_map(
        local, mesh=mesh, in_specs=placed, out_specs=P("ctx", "kvh"), check_vma=False
    )
```

time: 745 us -> 237 us (0.32)
  waiting for transfers between devices: 338 us -> 0 us
  Pallas kernels: 0 us -> 230 us
  local copies, waits for them, and re-layouts: 180 us -> 3.15 us
  matrix products: 110 us -> 0 us
  starting transfers between devices: 59.1 us -> 0 us
  other arithmetic: 30.9 us -> 0.69 us
  blocking collectives: 17.8 us -> 0 us
    pallas_call x0 -> x1, Pallas kernels: none -> 230 us  [exchange(): pl.pallas_call(kernel, out_shape=jax.ShapeDtypeStruct((ROWS, HEADS * HEAD...]
    ppermute x2 -> x0, waiting for transfers between devices: 174 us -> none  [from_behind(): return lax.ppermute(array, axis, pairs)]
    all_to_all x4 -> x0, waiting for transfers between devices: 164 us -> none  [the longest x1 156 us: local(): lax.all_to_all(outgoing, 'ctx', split_axis=0, concat_axis=0, tiled=True)]
    dot_general x35 -> x0, matrix products: 110 us -> none  [the longest x16 67.1 us: group_attend(): jnp.einsum('gqk,gkd->gqd', weights.astype(jnp.bfloat16), value_block, pre...]
    gather x35 -> x0, local copies, waits for them, and re-layouts: 99.8 us -> none  [the longest x16 47 us: group_attend(): value_block = jnp.take(table_v, index_part, axis=0)]
    all_to_all x4 -> x0, starting transfers between devices: 52.4 us -> none  [the longest x1 15.6 us: local(): lax.all_to_all(slot_meta, 'ctx', split_axis=0, concat_axis=0, tiled=True)]
    reshape x16 -> x1, local copies, waits for them, and re-layouts: 40.6 us -> 0.09 us  [local(): chosen = picks.reshape(HEADS * TOPK)]
    while x32 -> x0, local copies, waits for them, and re-layouts: 31.6 us -> none
  transfers between devices with their start and end apart: 6 -> 0, of which waited for: 3 -> 0; matrix products, arithmetic and copies ran while one was open for 8% -> 0% of each run, Pallas kernels for 0% -> 0%
where the time goes in v1:
time: 237 us; the launch traced here: 234 us
  Pallas kernels  230 us (97%)
  local copies, waits for them, and re-layouts  3.15 us (1%)
    pallas_call x1, Pallas kernels, exchange(): pl.pallas_call(kernel, out_shape=jax.ShapeDtypeStruct((ROWS, HEADS * HEAD...  230 us

profile of v1, /device:TPU:30, one launch (start us, length us, event | category | flops | bytes accessed | tf_op | source)
XLA Modules:
  0.0 234.0 jit_solution(3675028241620294685)
XLA Ops:
  0.0 0.8 copy.9
  0.8 0.1 reshape.95
  0.9 0.1 select_reduce_fusion
  1.0 0.6 pad_add_fusion
  1.5 230.2 %attend.1 = bf16[256,2048]{1,0:T(8,128)(2,1)} custom-call(bf16[256,2048]{1,0:T(8,128)(2,1)} %refs_0_.1, bf16[256,512]{1,0:T(8,128)(2,1)} %refs_1_.1, bf16[256,512]{1,0:T(8,128)(2,1)} %refs_2_.1, bf16[8,512,512]{2,1,0:T(8,128)(2,1)} %bitcast.3, bf16[8,512,512]{2,1,0:T(8,128)(2,1)} %bitcast.4, s32[1,256]{1,0:T(1,128)} %bitcast.5), custom_call_target="tpu_custom_call" | custom-call | tf_op jit(solution)/shard_map/attend/pallas_call | solution.py:516
  231.7 2.3 copy.11
  (1 shorter events, 0.0 us)
